TPU v7x, 32 devices: a whole 2x2x4 slice. The times are simulated.
32 devices in a mesh: row: 8 (over y, x, core), col: 4 (over z).
Axes of the slice: x: 2, y: 2, z: 4, core: 2. Of those that a mesh axis runs over, the one named last changes fastest.
Arguments:
- amplitudes: bfloat16 [6144, 3072], P('row', 'col'), may hold values from -6 to 6
- integrals: bfloat16 [4, 768, 6144], P(None, 'row', 'col'), may hold values from -0.109375 to 0.109375
- residual_in: bfloat16 [6144, 6144], P('row', 'col'), may hold values from -3 to 3
- pair_class: int32 [64], P('row'), may hold values from 0 to 1
- cd_class: int32 [32], replicated, may hold values from 0 to 1
- ab_class: int32 [64], P('col'), may hold values from 0 to 1
Outputs:
- residual_out: bfloat16 [6144, 6144], P('row', 'col')
All inputs are finite; a program needn't handle non-finite values.
Results may differ from a plain program's by a relative error of at most 0.001.
Values may be sent and summed in bfloat16 or wider, within the bound.
A program may use at most 128 MiB of HBM per device.

v0:
```python
import functools

import jax
import jax.numpy as jnp
from jax import lax
from jax.experimental import pallas as pl
from jax.experimental.pallas import tpu as pltpu
from jax.sharding import PartitionSpec as P

TILE = 96
HALVES = 2
BASE = 4
BLOCK = 256
COLS = 512
MESH = pl.DeviceIdType.MESH


def kernel(pair_ref, cd_ref, ab_ref, amp_ref, int_ref, res_ref, out_ref,
           slabs, pool_in, pool_out, pool_int, pool_select, panel, paired_int, select, masked, total, res_v, pair_col, cd_col, ab_lane,
           local_sem, int_send, int_recv, amp_send, amp_recv, pool_send, pool_recv):
    r = lax.axis_index("row")
    z = lax.axis_index("col")
    last = 3
    core, x, y = lax.rem(r, 2), lax.rem(r // 2, 2), r // 4
    x_nbr, y_nbr, sib = r + 2 - 4 * x, r + 4 - 8 * y, r + 1 - 2 * core
    diag = y_nbr + 2 - 4 * x
    is_mid = jnp.logical_and(z > 0, z < last)
    far = jnp.where(z == 1, 3, 0)
    far_to = jnp.where(z == 1, 0, 3)
    groups, width, columns = panel.shape
    tiles = width // TILE
    rows = amp_ref.shape[0]
    packed = slabs.shape[1]
    half = packed // HALVES
    pooled = pool_in.shape[1]
    cols = COLS if pooled <= COLS else COLS // 2
    def order(w):
        near = jnp.where(w == 1, z - 1, jnp.where(w == 2, z + 1, far))
        there = jnp.where(z == 0, w, jnp.where(z == last, last - w, near))
        return jnp.where(w == 0, z, there)

    barrier = pltpu.get_barrier_semaphore()
    for neighbour in (x_nbr, y_nbr, sib):
        pl.semaphore_signal(barrier, inc=1, device_id={"row": neighbour}, device_id_type=MESH)

    @pl.when(z > 0)
    def _():
        pl.semaphore_signal(barrier, inc=1, device_id={"col": z - 1}, device_id_type=MESH)

    @pl.when(z < last)
    def _():
        pl.semaphore_signal(barrier, inc=1, device_id={"col": z + 1}, device_id_type=MESH)

    def rows_of(owner):
        return pl.ds(pl.multiple_of(owner * TILE, TILE), TILE)

    def send_int(owner, wave, kind, to, own=False, side=None):
        g = order(wave)
        if side is None:
            there = panel.at[g, rows_of(owner), :]
        else:
            there = panel.at[g, rows_of(owner), pl.ds(side * (columns // 2), columns // 2)]
        return pltpu.make_async_remote_copy(
            src_ref=int_ref.at[g] if own else there,
            dst_ref=there,
            send_sem=int_send.at[kind, wave],
            recv_sem=int_recv.at[kind, wave],
            device_id={"row": to},
            device_id_type=MESH,
        )

    def own_x(w):
        return send_int(r, w, 0, x_nbr, own=True)

    def own_y(w):
        return send_int(r, w, 1, y_nbr, own=True)

    def fwd_y(w):
        return send_int(x_nbr, w, 2, y_nbr, side=0)

    def fwd_x(w):
        return send_int(y_nbr, w, 3, x_nbr, side=1)

    def to_sib(w, kind):
        return send_int((r, x_nbr, y_nbr, diag)[kind - 4], w, kind, sib, own=kind == 4)

    def recv_int(w, kind):
        owner = (x_nbr, y_nbr, diag, diag, sib, sib + 2 - 4 * x, sib + 4 - 8 * y, sib + 2 - 4 * x + 4 - 8 * y)[kind]
        send_int(owner, w, kind, sib, side={2: 0, 3: 1}.get(kind)).wait_recv()

    def slab(j, h):
        return slabs.at[j, pl.ds(pl.multiple_of(h * half, 16), half), :]

    def send_amp(j, h, send_at, to):
        return pltpu.make_async_remote_copy(
            src_ref=slab(j, h),
            dst_ref=slab(j, h),
            send_sem=amp_send.at[send_at],
            recv_sem=amp_recv.at[j, h],
            device_id={"col": to},
            device_id_type=MESH,
        )

    keep = pltpu.make_async_copy(int_ref, panel.at[:, rows_of(r), :], local_sem.at[0])
    prior = pltpu.make_async_copy(res_ref, res_v, local_sem.at[1])

    pl.semaphore_wait(barrier, 3 + (z > 0).astype(jnp.int32) + (z < last).astype(jnp.int32))

    for w in (0, 1):
        own_x(w).start()
        own_y(w).start()
    keep.start()

    def lane_labels(ref, base, count):
        lane = lax.broadcasted_iota(jnp.int32, (1, count * TILE), 1)
        labels = jnp.zeros_like(lane)
        for t in range(count):
            labels = jnp.where(lane >= t * TILE, ref[base + t], labels)
        return labels

    count_ones = []
    for g in range(groups):
        ones = jnp.int32(0)
        for t in range(tiles):
            ones = ones + cd_ref[g * tiles + t]
        count_ones.append(ones)

    def places(j, way):
        lane = lax.broadcasted_iota(jnp.int32, (1, width), 1)
        offsets = [jnp.int32(0), jnp.int32(0)]
        for g in range(groups):
            counted = jnp.logical_and(g >= way, g < j)
            for label, count in ((0, tiles - count_ones[g]), (1, count_ones[g])):
                offsets[label] += jnp.where(counted, jnp.maximum(count - BASE, 0), 0)
        place = jnp.zeros_like(lane)
        pool_place = jnp.zeros_like(lane)
        ones = jnp.int32(0)
        for t in range(tiles):
            label = cd_ref[j * tiles + t]
            rank = jnp.where(label == 1, ones, t - ones)
            left_over = rank - BASE + jnp.where(label == 1, offsets[1], offsets[0])
            left_over = jnp.where(rank >= BASE, left_over, -tiles)
            place = jnp.where(lane >= t * TILE, lane + (rank - t) * TILE, place)
            pool_place = jnp.where(lane >= t * TILE, lane + (left_over - t) * TILE, pool_place)
            ones = ones + label
        return place, pool_place

    def fill(target, place):
        slot = lax.broadcasted_iota(jnp.int32, target.shape, 0)
        target[...] = jnp.where(slot == place, 1.0, 0.0).astype(jnp.bfloat16)

    for t in range(rows // TILE):
        pair_col[pl.ds(t * TILE, TILE), :] = jnp.full((TILE, 1), pair_ref[t], jnp.int32)
    fill(select, places(z, 0)[0])
    own_labels = lane_labels(cd_ref, z * tiles, tiles)

    @pl.loop(0, rows // BLOCK)
    def _(i):
        span = pl.ds(pl.multiple_of(i * BLOCK, BLOCK), BLOCK)
        kept = jnp.where(pair_col[span, :] == own_labels, amp_ref[span, :].astype(jnp.float32), 0.0)
        masked[span, :] = kept.astype(jnp.bfloat16)

    for h in range(HALVES):
        @pl.loop(0, rows // BLOCK)
        def _(i, h=h):
            span = pl.ds(pl.multiple_of(i * BLOCK, BLOCK), BLOCK)
            tile = lax.dot_general(
                select[pl.ds(h * half, half), :], masked[span, :],
                (((1,), (1,)), ((), ())), preferred_element_type=jnp.float32,
            )
            slabs[z, pl.ds(h * half, half), span] = tile.astype(jnp.bfloat16)

        @pl.when(z > 0)
        def _(h=h):
            send_amp(z, h, h, z - 1).start()

        @pl.when(z < last)
        def _(h=h):
            send_amp(z, h, 2 + h, z + 1).start()

    for w in range(groups):
        to_sib(w, 4).start()
    prior.start()

    def send_pool(way):
        return pltpu.make_async_remote_copy(
            src_ref=pool_out.at[way],
            dst_ref=pool_in.at[way],
            send_sem=pool_send.at[way],
            recv_sem=pool_recv.at[way],
            device_id={"col": z + 1 - 2 * way},
            device_id_type=MESH,
        )

    @pl.loop(0, 2)
    def _(way):
        fill(pool_select, places(z, way)[1])

        @pl.loop(0, rows // BLOCK)
        def _(i):
            span = pl.ds(pl.multiple_of(i * BLOCK, BLOCK), BLOCK)
            pool_out[way, :, span] = lax.dot_general(
                pool_select[...], masked[span, :],
                (((1,), (1,)), ((), ())), preferred_element_type=jnp.float32,
            ).astype(jnp.bfloat16)

    @pl.when(z == 0)
    def _():
        send_pool(0).start()
        pool_in[0] = jnp.zeros_like(pool_in[0])

    @pl.when(z == last)
    def _():
        send_pool(1).start()
        pool_in[1] = jnp.zeros_like(pool_in[1])

    def pass_pool(way):
        send_pool(way).wait_recv()
        pool_out[way] = pool_out[way] + pool_in[way]
        send_pool(way).start()

    pool_int[...] = jnp.zeros_like(pool_int)
    for g in range(groups):
        for t in range(tiles):
            cd_col[g, pl.ds(t * TILE, TILE), :] = jnp.full((TILE, 1), cd_ref[g * tiles + t], jnp.int32)
    ab_lane[...] = lane_labels(ab_ref, 0, columns // TILE)

    def pass_on(j, h, send_at, to):
        copy = send_amp(j, h, send_at, to)
        copy.wait_recv()
        copy.start()

    def pass_near(h):
        @pl.when(is_mid)
        def _():
            pass_on(z - 1, h, 4 + h, z + 1)
            pass_on(z + 1, h, 6 + h, z - 1)

    def pass_far(h):
        @pl.when(is_mid)
        def _():
            pass_on(far, h, 8 + h, far_to)

    def take_wave(w):
        recv_int(w, 0)
        fwd_y(w).start()
        recv_int(w, 1)
        fwd_x(w).start()

        @pl.when(w + 2 < groups)
        def _():
            own_x(w + 2).start()
            own_y(w + 2).start()

        to_sib(w, 5).start()
        to_sib(w, 6).start()

    def take_diag(w):
        recv_int(w, 2)
        recv_int(w, 3)
        to_sib(w, 7).start()

    def pair_up(w):
        j = order(w)
        way = (j > z).astype(jnp.int32)
        place, pool_place = places(j, way)
        fill(select, place)
        fill(pool_select, pool_place)

        @pl.loop(0, columns // cols)
        def _(c):
            at = pl.ds(pl.multiple_of(c * cols, cols), cols)
            part = jnp.where(cd_col[j] == ab_lane[:, at], panel[j, :, at].astype(jnp.float32), 0.0)
            part = part.astype(jnp.bfloat16)
            paired_int[:, at] = jnp.dot(
                select[...], part, preferred_element_type=jnp.float32
            ).astype(jnp.bfloat16)
            extra = jnp.dot(pool_select[...], part, preferred_element_type=jnp.float32)
            pool_int[way, :, at] = pool_int[way, :, at] + extra.astype(jnp.bfloat16)

    def wait_amp(w, h):
        @pl.when(jnp.logical_not(is_mid))
        def _():
            send_amp(order(w), h, 0, 0).wait_recv()

    def multiply(left_of, right, store):
        @pl.loop(0, rows // BLOCK)
        def _(i):
            span = pl.ds(pl.multiple_of(i * BLOCK, BLOCK), BLOCK)
            left = left_of(span)

            @pl.loop(0, columns // cols)
            def _(c):
                at = pl.ds(pl.multiple_of(c * cols, cols), cols)
                store(span, at, jnp.dot(left, right[:, at], preferred_element_type=jnp.float32))

    def put(span, at, value):
        total[span, at] = value

    def multiply_slab(w):
        multiply(lambda span: slabs[order(w), :, span].T, paired_int, add)

    def add(span, at, value):
        total[span, at] += value

    def finish(span, at, value):
        ladder = jnp.where(pair_col[span, :] == ab_lane[:, at], total[span, at] + value, 0.0)
        out_ref[span, at] = (res_v[span, at].astype(jnp.float32) + ladder).astype(jnp.bfloat16)

    pass_near(0)
    take_wave(0)
    pass_near(1)
    keep.wait()

    @pl.loop(0, groups - 1)
    def _(w):
        @pl.when(w > 0)
        def _():
            pass_far(w - 1)

        @pl.when(jnp.logical_and(w == 2, is_mid))
        def _():
            pass_pool(z - 1)

        take_wave(w + 1)
        take_diag(w)
        for kind in (4, 5, 6, 7):
            recv_int(w, kind)

        @pl.when(w == 0)
        def _():
            multiply(lambda span: masked[span, :], panel.at[z], put)

        @pl.when(w > 0)
        def _():
            pair_up(w)
            for h in range(HALVES):
                wait_amp(w, h)
            multiply_slab(w)

    take_diag(last)

    @pl.when(is_mid)
    def _():
        pass_pool(2 - z)

    for kind in (4, 5, 6, 7):
        recv_int(last, kind)
    pair_up(last)
    for h in range(HALVES):
        wait_amp(last, h)
    multiply_slab(last)
    prior.wait()

    @pl.when(jnp.logical_not(is_mid))
    def _():
        send_pool((z == 0).astype(jnp.int32)).wait_recv()

    multiply(
        lambda span: pool_in[:, :, span].reshape(2 * pooled, BLOCK).T,
        pool_int.reshape(2 * pooled, columns),
        finish,
    )

    for w in range(groups):
        for copy in (own_x, own_y, fwd_y, fwd_x):
            copy(w).wait_send()
        for kind in (4, 5, 6, 7):
            to_sib(w, kind).wait_send()
    for h in range(HALVES):
        @pl.when(z > 0)
        def _(h=h):
            send_amp(z, h, h, z - 1).wait_send()

        @pl.when(z < last)
        def _(h=h):
            send_amp(z, h, 2 + h, z + 1).wait_send()

        @pl.when(is_mid)
        def _(h=h):
            send_amp(z - 1, h, 4 + h, z + 1).wait_send()
            send_amp(z + 1, h, 6 + h, z - 1).wait_send()
            send_amp(far, h, 8 + h, far_to).wait_send()

    @pl.when(z < last)
    def _():
        send_pool(0).wait_send()

    @pl.when(z > 0)
    def _():
        send_pool(1).wait_send()


def call(slots, ident, pair_class, cd_class, ab_class, amplitudes, integrals, residual_in):
    rows, width = amplitudes.shape
    groups, _, columns = integrals.shape
    smem = pl.BlockSpec(memory_space=pltpu.SMEM)
    vmem = pl.BlockSpec(memory_space=pltpu.VMEM)
    hbm = pl.BlockSpec(memory_space=pl.ANY)
    packed = BASE * TILE
    pooled = slots * TILE
    return pl.pallas_call(
        kernel,
        out_shape=jax.ShapeDtypeStruct((rows, columns), jnp.bfloat16),
        in_specs=[smem] * 3 + [vmem] + [hbm] * 2,
        out_specs=vmem,
        scratch_shapes=[
            pltpu.VMEM((groups, packed, rows), jnp.bfloat16),
            pltpu.VMEM((2, pooled, rows), jnp.bfloat16),
            pltpu.VMEM((2, pooled, rows), jnp.bfloat16),
            pltpu.VMEM((2, pooled, columns), jnp.bfloat16),
            pltpu.VMEM((pooled, width), jnp.bfloat16),
            pltpu.VMEM((groups, width, columns), jnp.bfloat16),
            pltpu.VMEM((packed, columns), jnp.bfloat16),
            pltpu.VMEM((packed, width), jnp.bfloat16),
            pltpu.VMEM((rows, width), jnp.bfloat16),
            pltpu.VMEM((rows, columns), jnp.float32),
            pltpu.VMEM((rows, columns), jnp.bfloat16),
            pltpu.VMEM((rows, 1), jnp.int32),
            pltpu.VMEM((groups, width, 1), jnp.int32),
            pltpu.VMEM((1, columns), jnp.int32),
            pltpu.SemaphoreType.DMA((2,)),
            pltpu.SemaphoreType.DMA((8, groups)),
            pltpu.SemaphoreType.DMA((8, groups)),
            pltpu.SemaphoreType.DMA((10,)),
            pltpu.SemaphoreType.DMA((groups, HALVES)),
            pltpu.SemaphoreType.DMA((2,)),
            pltpu.SemaphoreType.DMA((2,)),
        ],
        compiler_params=pltpu.CompilerParams(
            collective_id=ident, has_side_effects=True, vmem_limit_bytes=56 * 1024 * 1024,
        ),
        cost_estimate=pl.CostEstimate(
            flops=2 * rows * width * groups * columns, bytes_accessed=2 * rows * columns * 3, transcendentals=0,
        ),
        name=f"ladder_{slots}",
    )(pair_class, cd_class, ab_class, amplitudes, integrals, residual_in)


def paired(amplitudes, integrals, residual_in, pair_class, cd_class, ab_class):
    groups = integrals.shape[0]
    per_group = amplitudes.shape[1] // TILE
    ones = jnp.sum(cd_class.reshape(groups, per_group), axis=1)
    left_over = jnp.maximum(jnp.stack([ones, per_group - ones]) - BASE, 0)
    slots = jnp.max(jnp.sum(left_over, axis=1) - jnp.minimum(left_over[:, 0], left_over[:, -1]))
    sizes = (2, 3, 5, (groups - 1) * (per_group - BASE))
    branches = [functools.partial(call, size, ident) for ident, size in enumerate(sizes)]
    which = sum((slots > size).astype(jnp.int32) for size in sizes[:-1])
    return lax.switch(which, branches, pair_class, cd_class, ab_class, amplitudes, integrals, residual_in)


def from_behind(value, axis, steps):
    count = lax.axis_size(axis)
    pairs = [(source, (source + steps) % count) for source in range(count)]
    return lax.ppermute(value, axis, pairs)


def ringed(amplitudes, integrals, residual_in, pair_class, cd_class, ab_class):
    pair_labels = jnp.repeat(pair_class, TILE)
    cd_labels = jnp.repeat(cd_class, TILE)
    ab_labels = jnp.repeat(ab_class, TILE)
    nothing = jnp.zeros((), jnp.bfloat16)
    slab_width = amplitudes.shape[1]

    def mask_amp(values, offset):
        labels = lax.dynamic_slice_in_dim(cd_labels, offset, values.shape[1])
        return jnp.where(pair_labels[:, None] == labels[None, :], values, nothing)

    def mask_int(values, offset):
        labels = lax.dynamic_slice_in_dim(cd_labels, offset, values.shape[0])
        return jnp.where(labels[:, None] == ab_labels[None, :], values, nothing)

    initial = residual_in.astype(jnp.float32)
    col_count = lax.axis_size("col")
    col_index = lax.axis_index("col")

    def contribute(ladder_sum, amp_slab, group_id):
        own_part = lax.dynamic_index_in_dim(integrals, group_id, 0, keepdims=False)
        int_panel = lax.all_gather(own_part, "row", axis=0, tiled=True)
        offset = group_id * slab_width
        return ladder_sum + jnp.dot(
            mask_amp(amp_slab, offset),
            mask_int(int_panel, offset),
            preferred_element_type=jnp.float32,
        )

    ladder_sum = contribute(initial, amplitudes, col_index)

    def advance(counter, state_pair):
        running, amp_slab = state_pair
        amp_slab = from_behind(amp_slab, "col", 1)
        group_id = (col_index - counter) % col_count
        return (contribute(running, amp_slab, group_id), amp_slab)

    ladder_sum, _ = lax.fori_loop(1, col_count, advance, (ladder_sum, amplitudes))
    return ladder_sum.astype(jnp.bfloat16)


def solution(mesh):
    local = paired if (mesh.shape["row"], mesh.shape["col"]) == (8, 4) else ringed
    return jax.shard_map(
        local,
        mesh=mesh,
        in_specs=(P("row", "col"), P(None, "row", "col"), P("row", "col"), P("row"), P(), P("col")),
        out_specs=P("row", "col"),
        check_vma=False,
    )
```

profile of v0, /device:TPU:0, one launch (start us, length us, event | category | flops | bytes accessed | tf_op | source)
XLA Modules:
  0.0 87.5 jit_solution(17198502711231389443)
XLA Ops:
  0.0 0.7 reshape.11
  0.7 0.1 reduce_sum.18
  0.9 0.1 fusion.1
  1.0 0.2 minimum_reduce_fusion
  1.2 0.6 subtract_reduce_fusion
  3.8 82.3 %conditional.1 = (bf16[768,1536]{1,0:T(8,128)(2,1)S(1)}) conditional(s32[]{:T(128)} %clamp.3, (s32[8]{0:T(128)}, s32[32]{0:T(128)}, s32[16]{0:T(128)}, bf16[768,768]{1,0:T(8,128)(2,1)}, bf16[4,96,1536]{2,1,0:T(8,128)(2,1)}, /*index=5*/bf16[768,1536]{1,0:T(8,128)(2,1)}) %tuple.17, (s32[8]{0:T(128)}, s32[32]{0:T(128)}, ...), branch_computations={%region_3.0_spmd, %region_4.0_spmd, %region_5.0_spmd, %region_6.0_... | conditional | flops 7247757312 | bytes 7077896 | solution.py:449
  3.8 81.9 %ladder_5.1 = bf16[768,1536]{1,0:T(8,128)(2,1)S(1)} custom-call(s32[8]{0:T(128)} %get-tuple-element.70.pair_ref, s32[32]{0:T(128)} %get-tuple-element.71.cd_ref, s32[16]{0:T(128)} %get-tuple-element.72.ab_ref, bf16[768,768]{1,0:T(8,128)(2,1)} %get-tuple-element.73.amp_ref, bf16[4,96,1536]{2,1,0:T(8,128)(2,1)} %get-tuple-element.74.int_ref, ...), custom_call_target="tpu_custom_call" | custom-call | flops 7247757312 | bytes 7077888 | tf_op jit(solution)/shard_map/cond/branch_2_fun/ladder_5/pallas_call | solution.py:402
  86.1 1.4 %copy.16 = bf16[768,1536]{1,0:T(8,128)(2,1)} copy(bf16[768,1536]{1,0:T(8,128)(2,1)S(1)} %get-tuple-element.82) | data formatting | bytes 4718592
  (1 shorter events, 0.0 us)
where the time goes:
time: 87.6 us; the launch traced here: 87.5 us
  Pallas kernels  81.9 us (93%)
  local copies, waits for them, and re-layouts  2.14 us (2%)
  between operations  1.96 us (2%)
  other arithmetic  1.08 us (1%)
    pallas_call x1, Pallas kernels, call(): pl.pallas_call(kernel, out_shape=jax.ShapeDtypeStruct((rows, columns), jn...  81.9 us

commit v1 on v0

--- a/solution.py
+++ b/solution.py
@@ -207,12 +207,10 @@
     @pl.when(z == 0)
     def _():
         send_pool(0).start()
-        pool_in[0] = jnp.zeros_like(pool_in[0])
 
     @pl.when(z == last)
     def _():
         send_pool(1).start()
-        pool_in[1] = jnp.zeros_like(pool_in[1])
 
     def pass_pool(way):
         send_pool(way).wait_recv()
@@ -312,17 +310,19 @@
     pass_near(1)
     keep.wait()
 
+    last_way = (z < 2).astype(jnp.int32)
+
+    def multiply_pool(way, store):
+        multiply(lambda span: pool_in[way, :, span].T, pool_int.at[way], store)
+
     @pl.loop(0, groups - 1)
     def _(w):
-        @pl.when(w > 0)
-        def _():
-            pass_far(w - 1)
-
-        @pl.when(jnp.logical_and(w == 2, is_mid))
-        def _():
-            pass_pool(z - 1)
-
         take_wave(w + 1)
+
+        @pl.when(w == 0)
+        def _():
+            pass_far(0)
+
         take_diag(w)
         for kind in (4, 5, 6, 7):
             recv_int(w, kind)
@@ -330,6 +330,11 @@
         @pl.when(w == 0)
         def _():
             multiply(lambda span: masked[span, :], panel.at[z], put)
+            pass_far(1)
+
+            @pl.when(is_mid)
+            def _():
+                pass_pool(1 - last_way)
 
         @pl.when(w > 0)
         def _():
@@ -338,15 +343,19 @@
                 wait_amp(w, h)
             multiply_slab(w)
 
+        @pl.when(jnp.logical_and(w == 1, is_mid))
+        def _():
+            pass_pool(last_way)
+
     take_diag(last)
-
-    @pl.when(is_mid)
-    def _():
-        pass_pool(2 - z)
-
     for kind in (4, 5, 6, 7):
         recv_int(last, kind)
     pair_up(last)
+
+    @pl.when(is_mid)
+    def _():
+        multiply_pool(1 - last_way, add)
+
     for h in range(HALVES):
         wait_amp(last, h)
     multiply_slab(last)
@@ -354,13 +363,9 @@
 
     @pl.when(jnp.logical_not(is_mid))
     def _():
-        send_pool((z == 0).astype(jnp.int32)).wait_recv()
-
-    multiply(
-        lambda span: pool_in[:, :, span].reshape(2 * pooled, BLOCK).T,
-        pool_int.reshape(2 * pooled, columns),
-        finish,
-    )
+        send_pool(last_way).wait_recv()
+
+    multiply_pool(last_way, finish)
 
     for w in range(groups):
         for copy in (own_x, own_y, fwd_y, fwd_x):
@@ -437,16 +442,38 @@
     )(pair_class, cd_class, ab_class, amplitudes, integrals, residual_in)
 
 
+def pool_sizes(groups, per_group):
+    return (2, 3, 5, (groups - 1) * (per_group - BASE))
+
+
+def choose(groups, per_group, cd_ref, which_ref):
+    needed = jnp.int32(0)
+    for label in (0, 1):
+        left_over = []
+        for g in range(groups):
+            count = jnp.int32(0)
+            for t in range(per_group):
+                count += (cd_ref[g * per_group + t] == label).astype(jnp.int32)
+            left_over.append(jnp.maximum(count - BASE, 0))
+        ends = jnp.minimum(left_over[0], left_over[-1])
+        needed = jnp.maximum(needed, sum(left_over) - ends)
+    sizes = pool_sizes(groups, per_group)
+    which_ref[0] = sum((needed > size).astype(jnp.int32) for size in sizes[:-1])
+
+
 def paired(amplitudes, integrals, residual_in, pair_class, cd_class, ab_class):
     groups = integrals.shape[0]
     per_group = amplitudes.shape[1] // TILE
-    ones = jnp.sum(cd_class.reshape(groups, per_group), axis=1)
-    left_over = jnp.maximum(jnp.stack([ones, per_group - ones]) - BASE, 0)
-    slots = jnp.max(jnp.sum(left_over, axis=1) - jnp.minimum(left_over[:, 0], left_over[:, -1]))
-    sizes = (2, 3, 5, (groups - 1) * (per_group - BASE))
-    branches = [functools.partial(call, size, ident) for ident, size in enumerate(sizes)]
-    which = sum((slots > size).astype(jnp.int32) for size in sizes[:-1])
-    return lax.switch(which, branches, pair_class, cd_class, ab_class, amplitudes, integrals, residual_in)
+    smem = pl.BlockSpec(memory_space=pltpu.SMEM)
+    which = pl.pallas_call(
+        functools.partial(choose, groups, per_group),
+        out_shape=jax.ShapeDtypeStruct((1,), jnp.int32),
+        in_specs=[smem],
+        out_specs=smem,
+        name="choose",
+    )(cd_class)
+    branches = [functools.partial(call, size, ident) for ident, size in enumerate(pool_sizes(groups, per_group))]
+    return lax.switch(which[0], branches, pair_class, cd_class, ab_class, amplitudes, integrals, residual_in)
 
 
 def from_behind(value, axis, steps):

time: 87.6 us -> 63.4 us (0.72)
  the two profiles are of different devices: /device:TPU:0 before, /device:TPU:9 now
where the time goes in v1:
time: 63.4 us; the launch traced here: 63.2 us
  Pallas kernels  60.9 us (96%)
  local copies, waits for them, and re-layouts  1.41 us (2%)
  between operations  0.67 us (1%)
    pallas_call x1, Pallas kernels, call(): pl.pallas_call(kernel, out_shape=jax.ShapeDtypeStruct((rows, columns), jn...  59.6 us
    unnamed x1, local copies, waits for them, and re-layouts  1.41 us
    pallas_call x1, Pallas kernels, paired(): pl.pallas_call(functools.partial(choose, groups, per_group), out_shape=ja...  1.28 us

profile of v1, /device:TPU:9, one launch (start us, length us, event | category | flops | bytes accessed | tf_op | source)
XLA Modules:
  0.0 63.2 jit_solution(9065649912888325000)
XLA Ops:
  0.0 1.3 %choose.1 = s32[1]{0:T(128)} custom-call(s32[32]{0:T(128)} %cd_ref.1), custom_call_target="tpu_custom_call" | custom-call | tf_op jit(solution)/shard_map/choose/pallas_call | solution.py:468
  1.9 59.8 %conditional.1 = (bf16[768,1536]{1,0:T(8,128)(2,1)S(1)}) conditional(s32[]{:T(128)} %bitcast, (s32[8]{0:T(128)}, s32[32]{0:T(128)}, s32[16]{0:T(128)}, bf16[768,768]{1,0:T(8,128)(2,1)}, bf16[4,96,1536]{2,1,0:T(8,128)(2,1)}, /*index=5*/bf16[768,1536]{1,0:T(8,128)(2,1)}) %tuple.17, (s32[8]{0:T(128)}, s32[32]{0:T(128)}, ...), branch_computations={%region_0.0_spmd, %region_1.0_spmd, %region_2.0_spmd, %region_3.0_... | conditional | flops 7247757312 | bytes 7077896 | solution.py:476
  2.0 59.6 %ladder_2.1 = bf16[768,1536]{1,0:T(8,128)(2,1)S(1)} custom-call(s32[8]{0:T(128)} %get-tuple-element.56.pair_ref, s32[32]{0:T(128)} %get-tuple-element.58.cd_ref, s32[16]{0:T(128)} %get-tuple-element.60.ab_ref, bf16[768,768]{1,0:T(8,128)(2,1)} %get-tuple-element.61.amp_ref, bf16[4,96,1536]{2,1,0:T(8,128)(2,1)} %get-tuple-element.62.int_ref, ...), custom_call_target="tpu_custom_call" | custom-call | flops 7247757312 | bytes 7077888 | tf_op jit(solution)/shard_map/cond/branch_0_fun/ladder_2/pallas_call | solution.py:407
  61.8 1.4 %copy.16 = bf16[768,1536]{1,0:T(8,128)(2,1)} copy(bf16[768,1536]{1,0:T(8,128)(2,1)S(1)} %get-tuple-element.82) | data formatting | bytes 4718592

commit v2 on v1

--- a/solution.py
+++ b/solution.py
@@ -182,12 +182,13 @@
         to_sib(w, 4).start()
     prior.start()
 
-    def send_pool(way):
+    def send_pool(way, h):
+        span = pl.ds(h * (pooled // HALVES), pooled // HALVES)
         return pltpu.make_async_remote_copy(
-            src_ref=pool_out.at[way],
-            dst_ref=pool_in.at[way],
-            send_sem=pool_send.at[way],
-            recv_sem=pool_recv.at[way],
+            src_ref=pool_out.at[way, span, :],
+            dst_ref=pool_in.at[way, span, :],
+            send_sem=pool_send.at[way, h],
+            recv_sem=pool_recv.at[way, h],
             device_id={"col": z + 1 - 2 * way},
             device_id_type=MESH,
         )
@@ -206,16 +207,20 @@
 
     @pl.when(z == 0)
     def _():
-        send_pool(0).start()
+        for h in range(HALVES):
+            send_pool(0, h).start()
 
     @pl.when(z == last)
     def _():
-        send_pool(1).start()
+        for h in range(HALVES):
+            send_pool(1, h).start()
 
     def pass_pool(way):
-        send_pool(way).wait_recv()
-        pool_out[way] = pool_out[way] + pool_in[way]
-        send_pool(way).start()
+        for h in range(HALVES):
+            span = pl.ds(h * (pooled // HALVES), pooled // HALVES)
+            send_pool(way, h).wait_recv()
+            pool_out[way, span, :] = pool_out[way, span, :] + pool_in[way, span, :]
+            send_pool(way, h).start()
 
     pool_int[...] = jnp.zeros_like(pool_int)
     for g in range(groups):
@@ -339,13 +344,14 @@
         @pl.when(w > 0)
         def _():
             pair_up(w)
+
+            @pl.when(jnp.logical_and(w == 2, is_mid))
+            def _():
+                pass_pool(last_way)
+
             for h in range(HALVES):
                 wait_amp(w, h)
             multiply_slab(w)
-
-        @pl.when(jnp.logical_and(w == 1, is_mid))
-        def _():
-            pass_pool(last_way)
 
     take_diag(last)
     for kind in (4, 5, 6, 7):
@@ -363,7 +369,8 @@
 
     @pl.when(jnp.logical_not(is_mid))
     def _():
-        send_pool(last_way).wait_recv()
+        for h in range(HALVES):
+            send_pool(last_way, h).wait_recv()
 
     multiply_pool(last_way, finish)
 
@@ -389,11 +396,13 @@
 
     @pl.when(z < last)
     def _():
-        send_pool(0).wait_send()
+        for h in range(HALVES):
+            send_pool(0, h).wait_send()
 
     @pl.when(z > 0)
     def _():
-        send_pool(1).wait_send()
+        for h in range(HALVES):
+            send_pool(1, h).wait_send()
 
 
 def call(slots, ident, pair_class, cd_class, ab_class, amplitudes, integrals, residual_in):
@@ -429,8 +438,8 @@
             pltpu.SemaphoreType.DMA((8, groups)),
             pltpu.SemaphoreType.DMA((10,)),
             pltpu.SemaphoreType.DMA((groups, HALVES)),
-            pltpu.SemaphoreType.DMA((2,)),
-            pltpu.SemaphoreType.DMA((2,)),
+            pltpu.SemaphoreType.DMA((2, HALVES)),
+            pltpu.SemaphoreType.DMA((2, HALVES)),
         ],
         compiler_params=pltpu.CompilerParams(
             collective_id=ident, has_side_effects=True, vmem_limit_bytes=56 * 1024 * 1024,

time: 63.4 us -> 65.8 us (1.038)
  the two profiles are of different devices: /device:TPU:9 before, /device:TPU:0 now
where the time goes in v2:
time: 65.8 us; the launch traced here: 65.3 us
  Pallas kernels  63 us (96%)
  local copies, waits for them, and re-layouts  1.41 us (2%)
  between operations  0.67 us (1%)
    pallas_call x1, Pallas kernels, call(): pl.pallas_call(kernel, out_shape=jax.ShapeDtypeStruct((rows, columns), jn...  61.7 us
    unnamed x1, local copies, waits for them, and re-layouts  1.41 us

profile of v2, /device:TPU:0, one launch (start us, length us, event | category | flops | bytes accessed | tf_op | source)
XLA Modules:
  0.0 65.3 jit_solution(10847847692696171535)
XLA Ops:
  0.0 1.3 %choose.1 = s32[1]{0:T(128)} custom-call(s32[32]{0:T(128)} %cd_ref.1), custom_call_target="tpu_custom_call" | custom-call | tf_op jit(solution)/shard_map/choose/pallas_call | solution.py:477
  1.9 62.0 %conditional.1 = (bf16[768,1536]{1,0:T(8,128)(2,1)S(1)}) conditional(s32[]{:T(128)} %bitcast, (s32[8]{0:T(128)}, s32[32]{0:T(128)}, s32[16]{0:T(128)}, bf16[768,768]{1,0:T(8,128)(2,1)}, bf16[4,96,1536]{2,1,0:T(8,128)(2,1)}, /*index=5*/bf16[768,1536]{1,0:T(8,128)(2,1)}) %tuple.17, (s32[8]{0:T(128)}, s32[32]{0:T(128)}, ...), branch_computations={%region_0.0_spmd, %region_1.0_spmd, %region_2.0_spmd, %region_3.0_... | conditional | flops 7247757312 | bytes 7077896 | solution.py:485
  2.0 61.7 %ladder_3.1 = bf16[768,1536]{1,0:T(8,128)(2,1)S(1)} custom-call(s32[8]{0:T(128)} %get-tuple-element.64.pair_ref, s32[32]{0:T(128)} %get-tuple-element.65.cd_ref, s32[16]{0:T(128)} %get-tuple-element.66.ab_ref, bf16[768,768]{1,0:T(8,128)(2,1)} %get-tuple-element.67.amp_ref, bf16[4,96,1536]{2,1,0:T(8,128)(2,1)} %get-tuple-element.68.int_ref, ...), custom_call_target="tpu_custom_call" | custom-call | flops 7247757312 | bytes 7077888 | tf_op jit(solution)/shard_map/cond/branch_1_fun/ladder_3/pallas_call | solution.py:416
  63.9 1.4 %copy.16 = bf16[768,1536]{1,0:T(8,128)(2,1)} copy(bf16[768,1536]{1,0:T(8,128)(2,1)S(1)} %get-tuple-element.82) | data formatting | bytes 4718592
